TPU v7x, 256 devices: a whole 4x4x8 slice. The times are simulated.
256 devices in a mesh: batch: 64 (over y, x, z_hi), chan: 4 (over z_lo, core).
Axes of the slice: x: 4, y: 4, z: 8 (z_hi: 4, z_lo: 2; z = z_hi * 2 + z_lo), core: 2. Of those that a mesh axis runs over, the one named last changes fastest.
Arguments:
- fine_inputs: bfloat16 [64, 32, 32, 512], P('batch'), may hold values from -6 to 6
- fine_upstream: bfloat16 [64, 32, 32, 512], P('batch', None, None, 'chan'), may hold values from -6 to 6
- fine_bank: bfloat16 [8, 9, 512, 512], P(None, None, 'batch', 'chan'), may hold values from -0.09375 to 0.09375
- fine_coefs: float32 [64, 8], replicated, may hold values from 0 to 1, as said below
- coarse_inputs: bfloat16 [64, 16, 16, 512], P('batch'), may hold values from -6 to 6
- coarse_upstream: bfloat16 [64, 16, 16, 512], P('batch', None, None, 'chan'), may hold values from -6 to 6
- coarse_bank: bfloat16 [8, 9, 512, 512], P(None, None, 'batch', 'chan'), may hold values from -0.09375 to 0.09375
- coarse_coefs: float32 [64, 8], replicated, may hold values from 0 to 1, as said below
Outputs:
- fine_delta: bfloat16 [64, 32, 32, 512], P('batch', None, None, 'chan')
- fine_update: float32 [8, 9, 512, 512], P(None, None, 'batch', 'chan')
- fine_logit: float32 [64, 8], P('batch')
- coarse_delta: bfloat16 [64, 16, 16, 512], P('batch', None, None, 'chan')
- coarse_update: float32 [8, 9, 512, 512], P(None, None, 'batch', 'chan')
- coarse_logit: float32 [64, 8], P('batch')
Inputs may be any that keep to these rules, and one draw needn't show every extreme that they name: Each row of fine_coefs is a softmax: positive entries that sum to one. Each row of coarse_coefs is a softmax: positive entries that sum to one.
All inputs are finite; a program needn't handle non-finite values.
Results may differ from a plain program's by a relative error of at most 0.01.
Values may be sent and summed in bfloat16 or wider, within the bound.
A program may use at most 128 MiB of HBM per device.

v0:
```python
import jax
import jax.numpy as jnp
from jax import lax
from jax.sharding import PartitionSpec as P

BANKS = 8
FINE_SIDE = 32
COARSE_SIDE = 16
HIGH = lax.Precision.HIGHEST


def shifted(padded, row_shift, col_shift, side):
    window = padded[:, row_shift : row_shift + side, col_shift : col_shift + side, :]
    return window.reshape(window.shape[0], side * side, window.shape[3])


def local_grads(inputs, upstream, kernels, side):
    samples_here = inputs.shape[0]
    pad_in = jnp.pad(inputs, ((0, 0), (1, 1), (1, 1), (0, 0)))
    pad_up = jnp.pad(upstream, ((0, 0), (1, 1), (1, 1), (0, 0)))
    flat_up = upstream.reshape(samples_here, side * side, upstream.shape[3])
    delta = jnp.zeros((samples_here, side * side, inputs.shape[3]), jnp.float32)
    grad_taps = []
    for row_shift in range(3):
        for col_shift in range(3):
            tap = 3 * row_shift + col_shift
            window_in = shifted(pad_in, row_shift, col_shift, side)
            window_up = shifted(pad_up, 2 - row_shift, 2 - col_shift, side)
            grad_taps.append(
                jnp.einsum("bpc,bpo->bco", window_in, flat_up, preferred_element_type=jnp.float32)
                / side
            )
            delta = delta + jnp.einsum(
                "bpo,bco->bpc", window_up, kernels[:, tap], preferred_element_type=jnp.float32
            )
    return (delta.reshape(samples_here, side, side, inputs.shape[3]), jnp.stack(grad_taps, axis=1))


def one_layer(inputs, upstream, bank_part, coefs, side):
    samples_here = inputs.shape[0]
    first_row = lax.axis_index("batch") * samples_here
    own_coefs = lax.dynamic_slice_in_dim(coefs, first_row, samples_here, 0)
    flat_bank = bank_part.reshape(BANKS, -1).astype(jnp.float32)
    bank_rows = lax.all_gather(bank_part, "batch", axis=2, tiled=True)
    flat_rows = bank_rows.reshape(bank_rows.shape[0], -1).astype(jnp.float32)
    mixed = jnp.dot(own_coefs, flat_rows, precision=HIGH)
    kernels = mixed.reshape((samples_here,) + bank_rows.shape[1:]).astype(jnp.bfloat16)
    delta, kernel_grad = local_grads(inputs, upstream, kernels, side)
    delta_total = lax.psum(delta.astype(jnp.bfloat16), "chan").astype(jnp.float32)
    width = delta.shape[3] // lax.axis_size("chan")
    delta_part = lax.dynamic_slice_in_dim(delta_total, lax.axis_index("chan") * width, width, 3)
    moved = lax.all_to_all(
        kernel_grad.astype(jnp.bfloat16), "batch", split_axis=2, concat_axis=0, tiled=True
    ).astype(kernel_grad.dtype)
    flat_grads = moved.reshape(moved.shape[0], -1)
    update = jnp.dot(coefs.T, flat_grads, precision=HIGH).reshape(bank_part.shape)
    dcoef_part = lax.dot_general(flat_grads, flat_bank, (((1,), (1,)), ((), ())), precision=HIGH)
    return (delta_part.astype(jnp.bfloat16), update, dcoef_part)


def logit_grads(coefs, totals, samples_here):
    first_row = lax.axis_index("batch") * samples_here
    own_coefs = lax.dynamic_slice_in_dim(coefs, first_row, samples_here, 0)
    own_totals = lax.dynamic_slice_in_dim(totals, first_row, samples_here, 0)
    return own_coefs * (own_totals - jnp.sum(own_coefs * own_totals, axis=1, keepdims=True))


def per_device(
    fine_inputs,
    fine_upstream,
    fine_bank,
    fine_coefs,
    coarse_inputs,
    coarse_upstream,
    coarse_bank,
    coarse_coefs,
):
    fine_delta, fine_update, fine_partial = one_layer(
        fine_inputs, fine_upstream, fine_bank, fine_coefs, FINE_SIDE
    )
    coarse_delta, coarse_update, coarse_partial = one_layer(
        coarse_inputs, coarse_upstream, coarse_bank, coarse_coefs, COARSE_SIDE
    )
    fine_total, coarse_total = lax.psum((fine_partial, coarse_partial), ("batch", "chan"))
    samples_here = fine_inputs.shape[0]
    fine_logit = logit_grads(fine_coefs, fine_total, samples_here)
    coarse_logit = logit_grads(coarse_coefs, coarse_total, samples_here)
    return (fine_delta, fine_update, fine_logit, coarse_delta, coarse_update, coarse_logit)


def solution(mesh):
    return jax.shard_map(
        per_device,
        mesh=mesh,
        in_specs=(
            P("batch", None, None, None),
            P("batch", None, None, "chan"),
            P(None, None, "batch", "chan"),
            P(),
            P("batch", None, None, None),
            P("batch", None, None, "chan"),
            P(None, None, "batch", "chan"),
            P(),
        ),
        out_specs=(
            P("batch", None, None, "chan"),
            P(None, None, "batch", "chan"),
            P("batch", None),
            P("batch", None, None, "chan"),
            P(None, None, "batch", "chan"),
            P("batch", None),
        ),
        check_vma=False,
    )
```

profile of v0, /device:TPU:1, one launch (start us, length us, event | category | flops | bytes accessed | tf_op | source)
XLA Modules:
  0.0 524.2 jit_solution(8585332356747162847)
XLA Ops:
  7.2 0.7 all-gather.5.cloned.1.call-update
  8.0 0.7 all-gather.3.cloned.1.call-update
  8.7 1.2 fusion.60
  12.3 2.2 copy.31
  14.5 15.2 %all-to-all-start.1 = ((bf16[1,9,512,128]{3,1,0,2:T(8,128)(2,1)}), bf16[1,9,512,128]{3,1,0,2:T(8,128)(2,1)S(1)}, u32[]{:S(2)}, u32[]{:S(2)}) async-start(bf16[1,9,512,128]{3,1,0,2:T(8,128)(2,1)} %copy.31), calls=%async_computation.1 | async-start | bytes 4194304 | tf_op jit(solution)/shard_map/all_to_all | solution.py:52
  30.3 0.5 fusion.76
  30.8 0.5 fusion.74
  31.4 0.5 fusion.72
  31.9 0.5 fusion.70
  32.5 0.5 fusion.68
  33.0 0.6 fusion.66
  33.6 0.5 fusion.64
  34.1 0.5 fusion.62
  34.7 2.2 copy.28
  36.9 51.0 %all-to-all-done.1 = bf16[1,9,512,128]{3,1,0,2:T(8,128)(2,1)S(1)} async-done(((bf16[1,9,512,128]{3,1,0,2:T(8,128)(2,1)}), bf16[1,9,512,128]{3,1,0,2:T(8,128)(2,1)S(1)}, u32[]{:S(2)}, u32[]{:S(2)}) %all-to-all-start.1) | async-done | bytes 1179680 | tf_op jit(solution)/shard_map/all_to_all | solution.py:52
  87.9 5.9 %all-to-all-start = ((bf16[1,9,512,128]{3,1,0,2:T(8,128)(2,1)}), bf16[1,9,512,128]{3,1,0,2:T(8,128)(2,1)}, u32[]{:S(2)}, u32[]{:S(2)}) async-start(bf16[1,9,512,128]{3,1,0,2:T(8,128)(2,1)} %copy.28), calls=%async_computation | async-start | bytes 4194304 | tf_op jit(solution)/shard_map/all_to_all | solution.py:52
  94.1 0.6 copy.41
  94.7 0.6 copy.40
  95.3 0.8 pad_slice_fusion.24
  96.1 1.3 pad_slice_fusion.16
  97.8 1.3 reshape.891
  99.1 48.8 %all-to-all-done = bf16[1,9,512,128]{3,1,0,2:T(8,128)(2,1)} async-done(((bf16[1,9,512,128]{3,1,0,2:T(8,128)(2,1)}), bf16[1,9,512,128]{3,1,0,2:T(8,128)(2,1)}, u32[]{:S(2)}, u32[]{:S(2)}) %all-to-all-start) | async-done | bytes 1179680 | tf_op jit(solution)/shard_map/all_to_all | solution.py:52
  148.0 2.0 copy.61
  150.0 0.5 reshape.858
  150.5 0.6 fusion.166
  151.1 80.3 %all-gather.5.cloned.1.call-done = bf16[8,9,512,128]{3,2,1,0:T(8,128)(2,1)} async-done(((bf16[8,9,8,128]{3,2,1,0:T(8,128)(2,1)}), bf16[8,9,512,128]{3,2,1,0:T(8,128)(2,1)}) %all-gather.5.cloned.1.call-update) | async-done | bytes 9437200 | tf_op jit(solution)/shard_map/all_gather | solution.py:44
  231.4 16.2 %copy.58 = bf16[1,8,4608,128]{3,1,2,0:T(8,128)(2,1)S(1)} copy(bf16[1,8,4608,128]{3,2,1,0:T(8,128)(2,1)} %bitcast.537) | data formatting | bytes 18874368
  247.6 8.0 %fusion.146 = f32[1,9,512,128]{3,0,2,1:T(1,128)S(1)} fusion(bf16[9,512,128,8]{2,3,1,0:T(8,128)(2,1)S(1)} %bitcast.532, f32[1,8]{0,1:T(8,128)S(1)} %get-tuple-element.44), kind=kOutput, calls=%fused_computation.215 | convolution fusion | flops 56623104 | bytes 11796512 | tf_op jit(solution)/shard_map/dot_general | solution.py:46
  255.8 136.1 %all-gather.3.cloned.1.call-done = bf16[8,9,512,128]{3,2,1,0:T(8,128)(2,1)} async-done(((bf16[8,9,8,128]{3,2,1,0:T(8,128)(2,1)}), bf16[8,9,512,128]{3,2,1,0:T(8,128)(2,1)}) %all-gather.3.cloned.1.call-update) | async-done | bytes 9437200 | tf_op jit(solution)/shard_map/all_gather | solution.py:44
  391.9 16.2 %copy.59 = bf16[1,8,4608,128]{3,1,2,0:T(8,128)(2,1)S(1)} copy(bf16[1,8,4608,128]{3,2,1,0:T(8,128)(2,1)} %bitcast.536) | data formatting | bytes 18874368
  408.1 8.3 %fusion.148 = f32[1,9,512,128]{3,0,2,1:T(1,128)S(1)} fusion(bf16[9,512,128,8]{2,3,1,0:T(8,128)(2,1)S(1)} %bitcast.533, f32[1,8]{0,1:T(8,128)S(1)} %get-tuple-element.45), kind=kOutput, calls=%fused_computation.217 | convolution fusion | flops 56623104 | bytes 11796512 | tf_op jit(solution)/shard_map/dot_general | solution.py:46
  416.6 0.8 copy-done.9
  417.8 0.5 copy-done.8
  418.7 0.5 copy-done.7
  419.7 0.5 copy-done.6
  427.9 0.9 fusion.6
  428.8 1.9 fusion.4
  430.7 1.2 copy-done
  432.0 0.6 fusion.167
  432.5 0.8 copy.33
  433.3 0.8 copy.34
  435.0 76.0 %all-reduce.4 = (f32[64,8]{1,0:T(8,128)S(1)}, f32[64,8]{1,0:T(8,128)S(1)}) all-reduce(f32[64,8]{1,0:T(8,128)S(1)} %fusion.125, f32[64,8]{1,0:T(8,128)S(1)} %fusion.122), channel_id=1, replica_groups=mesh['batch'=64,'chan'=4] {'batch','chan'}, use_global_device_ids=true, to_apply=%region_1.2 | all-reduce | flops 1024 | bytes 8192 | tf_op jit(solution)/shard_map/psum | solution.py:84
  511.0 0.6 multiply_reduce_fusion
  511.6 0.6 multiply_reduce_fusion.1
  512.2 1.2 subtract_multiply_fusion
  513.3 1.2 subtract_multiply_fusion.1
  514.5 1.7 convert_convert_fusion
  516.2 1.5 convert_convert_fusion.1
  (87 shorter events, 13.6 us)
Async XLA Ops:
  7.2 2.8 copy-start.10
  7.2 2.7 copy-start.27
  7.2 224.2 %all-gather.5.cloned.1.call-start = ((), (), s32[]{:S(2)}) async-start(), calls=%async_computation.3 | async-start | bytes 9584640 | tf_op jit(solution)/shard_map/all_gather | solution.py:44
  7.9 384.0 %all-gather.3.cloned.1.call-start = ((), (), s32[]{:S(2)}) async-start(), calls=%async_computation.2 | async-start | bytes 9584640 | tf_op jit(solution)/shard_map/all_gather | solution.py:44
  14.5 15.3 %copy-start.1 = (bf16[1,32,32,128]{3,2,1,0:T(8,128)(2,1)S(1)}, bf16[1,32,32,128]{3,2,1,0:T(8,128)(2,1)}, u32[]{:S(2)}) copy-start(bf16[1,32,32,128]{3,2,1,0:T(8,128)(2,1)} %param.9) | copy-start | bytes 786436
  14.5 15.3 %copy-start.26 = (bf16[1,32,32,512]{3,2,1,0:T(8,128)(2,1)S(1)}, bf16[1,32,32,512]{3,2,1,0:T(8,128)(2,1)}, u32[]{:S(2)}) copy-start(bf16[1,32,32,512]{3,2,1,0:T(8,128)(2,1)} %param.8) | copy-start | bytes 3145732
  14.5 73.4 %all-to-all-start.1 = ((bf16[1,9,512,128]{3,1,0,2:T(8,128)(2,1)}), bf16[1,9,512,128]{3,1,0,2:T(8,128)(2,1)S(1)}, u32[]{:S(2)}, u32[]{:S(2)}) async-start(bf16[1,9,512,128]{3,1,0,2:T(8,128)(2,1)} %copy.31), calls=%async_computation.1 | async-start | bytes 4194304 | tf_op jit(solution)/shard_map/all_to_all | solution.py:52
  36.9 57.2 %copy-start.22 = (f32[64,8]{0,1:T(8,128)S(1)}, f32[64,8]{0,1:T(8,128)}, u32[]{:S(2)}) copy-start(f32[64,8]{0,1:T(8,128)} %param.11) | copy-start | bytes 6148
  36.9 57.2 %copy-start.23 = (f32[64,8]{0,1:T(8,128)S(1)}, f32[64,8]{0,1:T(8,128)}, u32[]{:S(2)}) copy-start(f32[64,8]{0,1:T(8,128)} %param.15) | copy-start | bytes 6148
  87.9 60.1 %all-to-all-start = ((bf16[1,9,512,128]{3,1,0,2:T(8,128)(2,1)}), bf16[1,9,512,128]{3,1,0,2:T(8,128)(2,1)}, u32[]{:S(2)}, u32[]{:S(2)}) async-start(bf16[1,9,512,128]{3,1,0,2:T(8,128)(2,1)} %copy.28), calls=%async_computation | async-start | bytes 4194304 | tf_op jit(solution)/shard_map/all_to_all | solution.py:52
  93.8 420.7 %all-reduce.8.cloned.1.call-start = ((), (), s32[]{:S(2)}) async-start(), calls=%async_computation.4 | async-start | bytes 2621440 | tf_op jit(solution)/shard_map/psum | solution.py:49
  416.4 1.0 copy-start.9
  417.3 0.9 copy-start.8
  418.3 0.9 copy-start.7
  419.2 0.9 copy-start.6
  420.2 0.9 copy-start.5
  421.1 0.9 copy-start.4
  422.1 0.9 copy-start.3
  423.0 0.9 copy-start.2
  424.0 0.8 copy-start.18
  424.0 1.1 copy-start.17
  424.4 0.9 copy-start.16
  425.1 0.8 copy-start.15
  425.3 0.8 copy-start.11
  425.9 0.8 copy-start.14
  426.2 0.8 copy-start.13
  426.8 0.8 copy-start.12
  427.0 0.8 copy-start.19
  430.7 1.3 copy-start
  431.9 2.1 copy-start.20
  433.3 1.2 copy-start.21
  434.5 76.4 %copy-start.25 = (f32[1,8]{1,0:T(1,128)S(1)}, f32[1,8]{1,0:T(1,128)}, u32[]{:S(2)}) copy-start(f32[1,8]{1,0:T(1,128)} %copy.41) | copy-start | bytes 100
  434.5 77.0 %copy-start.24 = (f32[1,8]{1,0:T(1,128)S(1)}, f32[1,8]{1,0:T(1,128)}, u32[]{:S(2)}) copy-start(f32[1,8]{1,0:T(1,128)} %copy.40) | copy-start | bytes 100
Sparse Core Ops, SparseCore 0:
  11.1 220.1 all-gather.4
  234.5 157.3 all-gather.2
  430.8 49.6 all-reduce.7
where the time goes:
time: 525 us; the launch traced here: 524 us
  waiting for transfers between devices  318 us (61%)
  blocking collectives  76 us (14%)
  local copies, waits for them, and re-layouts  53.3 us (10%)
  matrix products  34.7 us (7%)
  starting transfers between devices  21.4 us (4%)
  between operations  14.2 us (3%)
  other arithmetic  7.02 us (1%)
    all_gather x2, waiting for transfers between devices, one_layer(): bank_rows = lax.all_gather(bank_part, 'batch', axis=2, tiled=True)  216 us
    all_to_all x2, waiting for transfers between devices, one_layer(): lax.all_to_all(kernel_grad.astype(jnp.bfloat16), 'batch', split_axis=2, c...  99.9 us
    psum x1, blocking collectives, per_device(): lax.psum((fine_partial, coarse_partial), ('batch', 'chan'))  76 us
    unnamed x62, local copies, waits for them, and re-layouts  42.3 us
    all_to_all x2, starting transfers between devices, one_layer(): lax.all_to_all(kernel_grad.astype(jnp.bfloat16), 'batch', split_axis=2, c...  21.1 us
    dot_general x2, matrix products, one_layer(): mixed = jnp.dot(own_coefs, flat_rows, precision=HIGH)  16.3 us
  transfers between devices with their start and end apart: 5, of which 4 were waited for; matrix products, arithmetic and copies ran while one was open for 10% of the time, Pallas kernels for 0%

commit v1 on v0

--- a/solution.py
+++ b/solution.py
@@ -2,6 +2,7 @@
 import jax.numpy as jnp
 from jax import lax
 from jax.sharding import PartitionSpec as P
+from jax.lax import all_to_all, psum
 
 BANKS = 8
 FINE_SIDE = 32
@@ -41,7 +42,15 @@
     first_row = lax.axis_index("batch") * samples_here
     own_coefs = lax.dynamic_slice_in_dim(coefs, first_row, samples_here, 0)
     flat_bank = bank_part.reshape(BANKS, -1).astype(jnp.float32)
-    bank_rows = lax.all_gather(bank_part, "batch", axis=2, tiled=True)
+
+    def write_the_quarters(matrix, comm_axis):
+        z_new = psum(1, comm_axis)
+        tmp = jnp.stack(z_new * [matrix], 0)
+        odd = all_to_all(tmp, comm_axis, 0, 0)
+        side_arr = jnp.concatenate(odd, axis=2)
+        return side_arr
+
+    bank_rows = write_the_quarters(bank_part, "batch")
     flat_rows = bank_rows.reshape(bank_rows.shape[0], -1).astype(jnp.float32)
     mixed = jnp.dot(own_coefs, flat_rows, precision=HIGH)
     kernels = mixed.reshape((samples_here,) + bank_rows.shape[1:]).astype(jnp.bfloat16)

time: 525 us -> 838 us (1.60); the launches traced: 524 us -> 828 us
  blocking collectives: 76 us -> 468 us
  waiting for transfers between devices: 318 us -> 202 us
  local copies, waits for them, and re-layouts: 53.3 us -> 80.6 us
    all_gather x2 -> x0, waiting for transfers between devices: 216 us -> none  [one_layer(): bank_rows = lax.all_gather(bank_part, 'batch', axis=2, tiled=True)]
    all_to_all x0 -> x2, blocking collectives: none -> 214 us  [the longest x1 168 us: write_the_quarters(): odd = all_to_all(tmp, comm_axis, 0, 0)]
    psum x1, blocking collectives: 76 us -> 254 us  [per_device(): lax.psum((fine_partial, coarse_partial), ('batch', 'chan'))]
    all_to_all x0 -> x1, waiting for transfers between devices: none -> 158 us  [write_the_quarters(): odd = all_to_all(tmp, comm_axis, 0, 0)]
    all_to_all x2 -> x1, waiting for transfers between devices: 99.9 us -> 44.3 us  [one_layer(): lax.all_to_all(kernel_grad.astype(jnp.bfloat16), 'batch', split_axis=2, c...]
    reshape x0 -> x2, local copies, waits for them, and re-layouts: none -> 20.1 us  [write_the_quarters(): side_arr = jnp.concatenate(odd, axis=2)]
    all_to_all x2 -> x1, starting transfers between devices: 21.1 us -> 15.2 us  [one_layer(): lax.all_to_all(kernel_grad.astype(jnp.bfloat16), 'batch', split_axis=2, c...]
    unnamed x62 -> x72, local copies, waits for them, and re-layouts: 42.3 us -> 43.2 us
  transfers between devices with their start and end apart: 5 -> 3, of which waited for: 4 -> 2; matrix products, arithmetic and copies ran while one was open for 10% -> 7% of each run, Pallas kernels for 0% -> 0%
where the time goes in v1:
time: 838 us; the launch traced here: 828 us
  blocking collectives  468 us (56%)
  waiting for transfers between devices  202 us (24%)
  local copies, waits for them, and re-layouts  80.6 us (10%)
  matrix products  34.6 us (4%)
  starting transfers between devices  21.2 us (3%)
  between operations  14.9 us (2%)
    psum x1, blocking collectives, per_device(): lax.psum((fine_partial, coarse_partial), ('batch', 'chan'))  254 us
    all_to_all x1, blocking collectives, write_the_quarters(): odd = all_to_all(tmp, comm_axis, 0, 0)  168 us
    all_to_all x1, waiting for transfers between devices, write_the_quarters(): odd = all_to_all(tmp, comm_axis, 0, 0)  158 us
    all_to_all x1, blocking collectives, one_layer(): lax.all_to_all(kernel_grad.astype(jnp.bfloat16), 'batch', split_axis=2, c...  45.8 us
    all_to_all x1, waiting for transfers between devices, one_layer(): lax.all_to_all(kernel_grad.astype(jnp.bfloat16), 'batch', split_axis=2, c...  44.3 us
    unnamed x72, local copies, waits for them, and re-layouts  43.2 us
    reshape x2, local copies, waits for them, and re-layouts, write_the_quarters(): side_arr = jnp.concatenate(odd, axis=2)  20.1 us
  transfers between devices with their start and end apart: 3, of which 2 were waited for; matrix products, arithmetic and copies ran while one was open for 7% of the time, Pallas kernels for 0%

profile of v1, /device:TPU:1, one launch (start us, length us, event | category | flops | bytes accessed | tf_op | source)
XLA Modules:
  0.0 828.0 jit_solution(13533640267203988518)
XLA Ops:
  7.2 1.3 fusion.60
  10.9 2.2 copy.33
  13.1 15.2 %all-to-all-start.3 = ((bf16[1,9,512,128]{3,1,0,2:T(8,128)(2,1)}), bf16[1,9,512,128]{3,1,0,2:T(8,128)(2,1)S(1)}, u32[]{:S(2)}, u32[]{:S(2)}) async-start(bf16[1,9,512,128]{3,1,0,2:T(8,128)(2,1)} %copy.33), calls=%async_computation.3 | async-start | bytes 4194304 | tf_op jit(solution)/shard_map/all_to_all | solution.py:61
  28.8 0.5 fusion.76
  29.4 0.5 fusion.74
  29.9 0.5 fusion.72
  30.5 0.5 fusion.70
  31.0 0.5 fusion.68
  31.6 0.6 fusion.66
  32.1 0.5 fusion.64
  32.6 0.5 fusion.62
  33.2 2.2 copy.29
  35.4 44.3 %all-to-all-done.3 = bf16[1,9,512,128]{3,1,0,2:T(8,128)(2,1)S(1)} async-done(((bf16[1,9,512,128]{3,1,0,2:T(8,128)(2,1)}), bf16[1,9,512,128]{3,1,0,2:T(8,128)(2,1)S(1)}, u32[]{:S(2)}, u32[]{:S(2)}) %all-to-all-start.3) | async-done | bytes 1179680 | tf_op jit(solution)/shard_map/all_to_all | solution.py:61
  79.7 45.8 %all_to_all.40 = bf16[1,9,512,128]{3,1,0,2:T(8,128)(2,1)} all-to-all(bf16[1,9,512,128]{3,1,0,2:T(8,128)(2,1)} %copy.29), channel_id=1, replica_groups=mesh['batch'=64,'chan'=4] {'batch'}, dimensions={2} | all-to-all | bytes 2359296 | tf_op jit(solution)/shard_map/all_to_all | solution.py:61
  125.5 2.3 stack.55
  127.8 168.0 %all_to_all.41 = bf16[64,8,9,8,128]{4,3,2,1,0:T(8,128)(2,1)} all-to-all(bf16[64,8,9,8,128]{4,3,2,1,0:T(8,128)(2,1)S(1)} %stack.55), channel_id=1, replica_groups=mesh['batch'=64,'chan'=4] {'batch'}, dimensions={0} | all-to-all | bytes 18874368 | tf_op jit(solution)/shard_map/all_to_all | solution.py:49
  295.8 5.9 stack.44
  301.7 6.0 all-to-all-start
  307.8 0.6 copy.43
  308.4 0.6 copy.42
  309.0 0.8 pad_slice_fusion.24
  309.8 1.3 pad_slice_fusion.16
  311.5 1.4 reshape.895
  312.9 0.6 copy-done
  313.9 0.5 reshape.862
  314.4 0.6 fusion.166
  315.0 10.1 %copy.32 = bf16[8,9,64,8,128]{4,3,2,1,0:T(8,128)(2,1)} copy(bf16[8,9,64,8,128]{4,3,1,0,2:T(8,128)(2,1)} %bitcast.536) | data formatting | bytes 18874368 | tf_op jit(solution)/shard_map/reshape | solution.py:50
  325.0 16.2 %copy.60 = bf16[1,8,4608,128]{3,1,2,0:T(8,128)(2,1)S(1)} copy(bf16[1,8,4608,128]{3,2,1,0:T(8,128)(2,1)} %bitcast.537) | data formatting | bytes 18874368
  341.3 8.0 fusion.146
  349.5 157.5 %all-to-all-done = bf16[64,8,9,8,128]{4,3,2,1,0:T(8,128)(2,1)} async-done(((bf16[64,8,9,8,128]{4,3,2,1,0:T(8,128)(2,1)}), bf16[64,8,9,8,128]{4,3,2,1,0:T(8,128)(2,1)}, u32[]{:S(2)}, u32[]{:S(2)}) %all-to-all-start) | async-done | bytes 9437216 | tf_op jit(solution)/shard_map/all_to_all | solution.py:49
  507.0 10.0 %copy.27 = bf16[8,9,64,8,128]{4,3,2,1,0:T(8,128)(2,1)} copy(bf16[8,9,64,8,128]{4,3,1,0,2:T(8,128)(2,1)} %bitcast.4) | data formatting | bytes 18874368 | tf_op jit(solution)/shard_map/reshape | solution.py:50
  517.0 16.2 %copy.61 = bf16[1,8,4608,128]{3,1,2,0:T(8,128)(2,1)S(1)} copy(bf16[1,8,4608,128]{3,2,1,0:T(8,128)(2,1)} %bitcast.538) | data formatting | bytes 18874368
  533.3 8.0 fusion.148
  541.5 0.8 copy-done.12
  548.4 0.5 copy-done.5
  552.8 0.9 fusion.6
  553.7 1.9 fusion.4
  555.6 1.2 copy-done.1
  556.9 0.6 fusion.167
  557.4 0.8 copy.35
  558.2 0.8 copy.36
  560.0 254.0 %all-reduce.4 = (f32[64,8]{1,0:T(8,128)S(1)}, f32[64,8]{1,0:T(8,128)S(1)}) all-reduce(f32[64,8]{1,0:T(8,128)S(1)} %fusion.125, f32[64,8]{1,0:T(8,128)S(1)} %fusion.122), channel_id=1, replica_groups=mesh['batch'=64,'chan'=4] {'batch','chan'}, use_global_device_ids=true, to_apply=%region_1.2 | all-reduce | flops 1024 | bytes 8192 | tf_op jit(solution)/shard_map/psum | solution.py:93
  814.0 0.6 multiply_reduce_fusion
  814.7 0.6 multiply_reduce_fusion.1
  815.3 1.2 subtract_multiply_fusion
  816.4 1.2 subtract_multiply_fusion.1
  817.6 1.7 convert_convert_fusion
  819.3 1.5 convert_convert_fusion.1
  (97 shorter events, 14.9 us)
Async XLA Ops:
  7.2 1.3 copy-start.13
  7.2 1.3 copy-start.32
  13.1 15.3 %copy-start.4 = (bf16[1,32,32,128]{3,2,1,0:T(8,128)(2,1)S(1)}, bf16[1,32,32,128]{3,2,1,0:T(8,128)(2,1)}, u32[]{:S(2)}) copy-start(bf16[1,32,32,128]{3,2,1,0:T(8,128)(2,1)} %param.9) | copy-start | bytes 786436
  13.1 15.3 %copy-start.31 = (bf16[1,32,32,512]{3,2,1,0:T(8,128)(2,1)S(1)}, bf16[1,32,32,512]{3,2,1,0:T(8,128)(2,1)}, u32[]{:S(2)}) copy-start(bf16[1,32,32,512]{3,2,1,0:T(8,128)(2,1)} %param.8) | copy-start | bytes 3145732
  13.1 66.6 %all-to-all-start.3 = ((bf16[1,9,512,128]{3,1,0,2:T(8,128)(2,1)}), bf16[1,9,512,128]{3,1,0,2:T(8,128)(2,1)S(1)}, u32[]{:S(2)}, u32[]{:S(2)}) async-start(bf16[1,9,512,128]{3,1,0,2:T(8,128)(2,1)} %copy.33), calls=%async_computation.3 | async-start | bytes 4194304 | tf_op jit(solution)/shard_map/all_to_all | solution.py:61
  35.4 90.1 %copy-start.23 = (bf16[8,9,8,128]{3,2,1,0:T(8,128)(2,1)S(1)}, bf16[8,9,8,128]{3,2,1,0:T(8,128)(2,1)}, u32[]{:S(2)}) copy-start(bf16[8,9,8,128]{3,2,1,0:T(8,128)(2,1)} %param.14) | copy-start | bytes 442372
  127.8 168.0 %copy-start.25 = (bf16[8,9,8,128]{3,2,1,0:T(8,128)(2,1)S(1)}, bf16[8,9,8,128]{3,2,1,0:T(8,128)(2,1)}, u32[]{:S(2)}) copy-start(bf16[8,9,8,128]{3,2,1,0:T(8,128)(2,1)} %param.10) | copy-start | bytes 442372
  301.7 6.0 copy-start.27
  301.7 6.0 copy-start.28
  301.7 205.3 %all-to-all-start = ((bf16[64,8,9,8,128]{4,3,2,1,0:T(8,128)(2,1)}), bf16[64,8,9,8,128]{4,3,2,1,0:T(8,128)(2,1)}, u32[]{:S(2)}, u32[]{:S(2)}) async-start(bf16[64,8,9,8,128]{4,3,2,1,0:T(8,128)(2,1)} %stack.44), calls=%async_computation | async-start | bytes 18874368 | tf_op jit(solution)/shard_map/all_to_all | solution.py:49
  307.7 509.9 %all-reduce.8.cloned.1.call-start = ((), (), s32[]{:S(2)}) async-start(), calls=%async_computation.4 | async-start | bytes 2621440 | tf_op jit(solution)/shard_map/psum | solution.py:58
  311.5 2.0 copy-start
  314.4 10.6 %copy-start.2 = (bf16[64,9216]{1,0:T(8,128)(2,1)}, bf16[64,9216]{1,0:T(8,128)(2,1)S(1)}, u32[]{:S(2)}) copy-start(bf16[64,9216]{1,0:T(8,128)(2,1)S(1)} %reshape.862) | copy-start | bytes 3538948
  541.3 1.0 copy-start.12
  542.2 0.9 copy-start.11
  543.2 0.9 copy-start.10
  544.1 0.9 copy-start.9
  545.1 0.9 copy-start.8
  546.0 0.9 copy-start.7
  547.0 0.9 copy-start.6
  547.9 0.9 copy-start.5
  548.9 0.8 copy-start.21
  548.9 1.1 copy-start.20
  549.3 0.9 copy-start.19
  550.0 0.8 copy-start.18
  550.2 0.8 copy-start.14
  550.8 0.8 copy-start.17
  551.1 0.8 copy-start.16
  551.7 0.8 copy-start.15
  551.9 0.8 copy-start.22
  555.6 1.3 copy-start.1
  556.9 2.1 copy-start.24
  558.2 1.4 copy-start.3
  558.2 1.4 copy-start.26
  559.4 254.6 %copy-start.30 = (f32[1,8]{1,0:T(1,128)S(1)}, f32[1,8]{1,0:T(1,128)}, u32[]{:S(2)}) copy-start(f32[1,8]{1,0:T(1,128)} %copy.43) | copy-start | bytes 100
  559.4 255.2 %copy-start.29 = (f32[1,8]{1,0:T(1,128)S(1)}, f32[1,8]{1,0:T(1,128)}, u32[]{:S(2)}) copy-start(f32[1,8]{1,0:T(1,128)} %copy.42) | copy-start | bytes 100
Sparse Core Ops, SparseCore 0:
  555.7 227.9 all-reduce.7
